TPU v7x, 32 devices: a whole 2x2x4 slice. The times are simulated.
32 devices in a mesh: prow: 8 (over z, y), pcol: 4 (over x, core).
Axes of the slice: x: 2, y: 2, z: 4, core: 2. Of those that a mesh axis runs over, the one named last changes fastest.
Arguments:
- data: float32 [16384, 8192], P('prow', 'pcol'), may hold values from 0.05 to 5
- w_trans: float32 [32, 16384], P(None, ('prow', 'pcol')), as said below
- h_prior: float32 [32, 8192], P(None, 'pcol'), may hold values from 0.1 to 3
Outputs:
- h_next: float32 [32, 8192], P(None, 'pcol')
Inputs may be any that keep to these rules, and one draw needn't show every extreme that they name: `w_trans`: every entry is positive.
All inputs are finite; a program needn't handle non-finite values.
Results may differ from a plain program's by a relative error of at most 0.0003.
Values sent between devices are 32-bit elements; how exact they have to be, the bound alone decides.
No kernel may reach another device: no remote copies, remote signals or barrier semaphores. Data moves between devices by JAX's collectives and lax.ppermute only.
A program may use at most 64 MiB of HBM per device.

v0:
```python
import functools

import jax
import jax.numpy as jnp
from jax import lax
from jax.experimental import pallas as pl
from jax.experimental.pallas import tpu as pltpu
from jax.sharding import PartitionSpec as P

LANES = 128
GRAM_ROWS = 8
VMEM = pl.BlockSpec(memory_space=pltpu.VMEM)
HBM = pl.BlockSpec(memory_space=pltpu.HBM)


def call(kernel, out_shape, operands, name, mebibytes=4, in_specs=None, scratch=(), cost=None):
    many = isinstance(out_shape, list)
    return pl.pallas_call(
        kernel,
        out_shape=out_shape,
        in_specs=in_specs or [VMEM] * len(operands),
        out_specs=[VMEM] * len(out_shape) if many else VMEM,
        compiler_params=pltpu.CompilerParams(vmem_limit_bytes=mebibytes * 1024 * 1024),
        scratch_shapes=list(scratch),
        cost_estimate=cost,
        name=name,
    )(*operands)


def floats(*shape):
    return jax.ShapeDtypeStruct(shape, jnp.float32)


def split(value):
    high = value.astype(jnp.bfloat16)
    low = (value - high.astype(jnp.float32)).astype(jnp.bfloat16)
    return high, low


def exact_dot(left, right, dims):
    return lax.dot_general(
        left, right, (dims, ((), ())),
        precision=lax.Precision.HIGHEST, preferred_element_type=jnp.float32,
    )


def block_start(near, width, side_turn, level_turn):
    row_at = lax.axis_index("prow")
    side, level = lax.rem(row_at, near), lax.div(row_at, near)
    peer = (level ^ level_turn) * near + (side ^ side_turn)
    return pl.multiple_of(peer * width, width)


def row_part(depth, turn):
    return pl.ds(pl.multiple_of((lax.axis_index("pcol") ^ turn) * depth, depth), depth)


def start_copies(near, width, n_col, blocks, data_ref, out_ref, sems):
    depth = data_ref.shape[0] // n_col
    copies = {}
    for at, turn in blocks:
        columns = pl.ds(block_start(near, width, *at[1]), width)
        rows = row_part(depth, turn)
        copies[at[0], turn] = pltpu.make_async_copy(
            data_ref.at[rows, columns], out_ref.at[at[0], rows], sems.at[at[0], turn]
        )
        copies[at[0], turn].start()
    return copies


def split_basis(part_ref, out_ref, turn):
    rank = part_ref.shape[0]
    part = part_ref[...]
    high, low = split(part)
    out_ref[turn, :rank] = high
    out_ref[turn, rank:] = low
    return exact_dot(part, part, ((1,), (1,)))


def product(w_split, blocks, at, turns):
    rank, depth = w_split.shape[1] // 2, w_split.shape[2]
    total = None
    for turn in turns:
        high, low = split(blocks[at, row_part(depth, turn)])
        upper = jnp.dot(w_split[turn], high, preferred_element_type=jnp.float32)
        term = (
            upper[:rank]
            + upper[rank:]
            + jnp.dot(w_split[turn, :rank], low, preferred_element_type=jnp.float32)
        )
        total = term if total is None else total + term
    return total


def store(cross, out_ref, row, before=None):
    rank = cross.shape[0]
    for i in range(cross.shape[1] // LANES):
        rows = slice(row + rank * i, row + rank * (i + 1))
        piece = cross[:, LANES * i : LANES * (i + 1)]
        out_ref[rows] = piece if before is None else piece + before[rows]


def own_region(compute):
    pl.when(lax.axis_index("prow") >= 0)(compute)


def load_kernel(near, width, n_col, early, late, others, *refs):
    w_refs, data_ref = refs[: len(early)], refs[len(early)]
    blocks, begun, w_split, gram_ref, sems = refs[len(early) + 1 :]
    order = [(at, turn) for turn in early + late for at in enumerate(others)]
    copies = start_copies(near, width, n_col, order, data_ref, blocks, sems)

    def compute():
        gram = split_basis(w_refs[0], w_split, early[0])
        for turn, ref in list(zip(early, w_refs))[1:]:
            gram = gram + split_basis(ref, w_split, turn)
        gram_ref[...] = gram
        for at in range(len(others)):
            for turn in early:
                copies[at, turn].wait()
            store(product(w_split, blocks, at, early), begun.at[at], 0)

    own_region(compute)
    for (_, turn), copy in copies.items():
        if turn not in early:
            copy.wait()


def finish(slab, first, count, w_split, late, blocks, begun, gram, out_refs):
    for index, out_ref in enumerate(out_refs):
        for at in range(count):
            block = first + index * count + at
            store(
                product(w_split, blocks, block, late), out_ref.at[pl.ds(slab * at, slab)], 0,
                begun.at[block],
            )
        if gram is not None:
            out_ref[slab * count :] = gram


def first_kernel(slab, count, early, late, *refs):
    w_refs, (w_early, gram_early, blocks, begun) = refs[: len(late)], refs[len(late) :][:4]
    *out_refs, w_split, gram_ref = refs[len(late) + 4 :]
    rank = w_refs[0].shape[0]
    for turn in early:
        w_split[turn] = w_early[turn]
    gram = gram_early[...]
    for turn, ref in zip(late, w_refs):
        gram = gram + split_basis(ref, w_split, turn)
    slabs = [gram[GRAM_ROWS * i : GRAM_ROWS * (i + 1)] for i in range(rank // GRAM_ROWS)]
    packed = jnp.concatenate(slabs, axis=1)
    gram_ref[...] = packed
    finish(slab, 0, count, w_split, late, blocks, begun, packed, out_refs)


def second_kernel(near, width, n_col, slab, count, n_sides, late, owns, *refs):
    w_split, blocks, begun, data_ref = refs[:4]
    out_refs, own_refs, (own_blocks, sems) = refs[4 : 4 + n_sides], refs[4 + n_sides : -2], refs[-2:]
    order = [(at, turn) for at in enumerate(owns) for turn in range(n_col)]
    copies = start_copies(near, width, n_col, order, data_ref, own_blocks, sems)

    def compute():
        first = n_sides * count
        finish(slab, first, count, w_split, late, blocks, begun, None, out_refs)

    def multiply(at):
        for turn in range(n_col):
            copies[at, turn].wait()
        store(product(w_split, own_blocks, at, range(n_col)), own_refs[at], 0)

    own_region(compute)
    for at in range(len(owns)):
        own_region(functools.partial(multiply, at))


def side_sum_kernel(count, slab, n_got, gram_sent, *refs):
    own_refs, gram_ref, got_refs = refs[:count], refs[count], refs[count + 1 : count + 1 + n_got]
    out_refs = refs[count + 1 + n_got :]
    gram = gram_ref[...]
    if gram_sent:
        for got in got_refs:
            gram = gram + got[slab * count :]
        out_refs[count][...] = gram
    for at in range(count):
        total = own_refs[at][...]
        for got in got_refs:
            total = total + got[slab * at : slab * (at + 1)]
        out_refs[at][:slab] = total
        out_refs[at][slab:] = gram


def sweep_kernel(width, *refs):
    parts, h_ref, out_ref = refs[:-2], refs[-2], refs[-1]
    rank = h_ref.shape[0]
    row_at = lax.axis_index("prow")
    total = parts[0][...]
    for part in parts[1:]:
        total = total + part[...]
    pieces = width // LANES
    cross = jnp.concatenate([total[rank * i : rank * (i + 1)] for i in range(pieces)], axis=1)
    packed = total[rank * pieces :]
    gram = jnp.concatenate(
        [packed[:, rank * i : rank * (i + 1)] for i in range(rank // GRAM_ROWS)], axis=0
    )
    h = h_ref[:, pl.ds(pl.multiple_of(row_at * width, width), width)]
    rest = cross - exact_dot(gram, h, ((1,), (0,)))
    rows = []
    for k in range(rank):
        inverse = 1.0 / gram[k : k + 1, k : k + 1]
        old = h[k : k + 1]
        fresh = jnp.maximum(old + rest[k : k + 1] * inverse, 0.0)
        rows.append(fresh)
        rest = rest - gram[:, k : k + 1] * (fresh - old)
    done = jnp.concatenate(rows, axis=0)
    for peer in range(out_ref.shape[0]):
        out_ref[peer] = done


def assemble_kernel(width, pieces, out_ref):
    for peer in range(pieces.shape[0]):
        out_ref[:, width * peer : width * (peer + 1)] = pieces[peer]


def shards(n_row, n_col, data, w_trans, h_prior):
    rank, depth = w_trans.shape
    rows, cols = data.shape
    width = cols // n_row
    near = max(1, n_row // 4)
    far = n_row // near
    slab = rank * (width // LANES)
    groups = [list(range(far // 2, far)), list(range(far // 2 - 1, -1, -1))]
    count = far // 2
    sides = range(1, near)

    def permute(value, axis, turn):
        size = n_row if axis == "prow" else n_col
        return lax.ppermute(value, axis, [(i, i ^ turn) for i in range(size)])

    w_parts = [w_trans] + [permute(w_trans, "pcol", t) for t in range(1, n_col)]
    early = list(range(1, min(2, n_col)))
    late = [turn for turn in range(n_col) if turn not in early]
    others = [(side, turn) for group in groups for side in sides for turn in group]
    owns = [(0, turn) for group in groups for turn in group]
    split_parts = jax.ShapeDtypeStruct((n_col, 2 * rank, depth), jnp.bfloat16)
    outward = [floats(count * slab + GRAM_ROWS, LANES)] * len(sides)
    blocks, begun, w_early, gram_early = call(
        functools.partial(load_kernel, near, width, n_col, early, late, others),
        [
            floats(len(others), rows, width),
            floats(len(others), slab, LANES),
            split_parts,
            floats(rank, rank),
        ],
        [*(w_parts[t] for t in early), data], "load_other_side", 40,
        [VMEM] * len(early) + [HBM], [pltpu.SemaphoreType.DMA((len(others), n_col))],
        pl.CostEstimate(
            flops=0, bytes_accessed=8 * rows * width * len(others), transcendentals=0
        ),
    )
    *sent_first, w_split, gram = call(
        functools.partial(first_kernel, slab, count, early, late),
        [*outward, split_parts, floats(GRAM_ROWS, LANES)],
        [*(w_parts[t] for t in late), w_early, gram_early, blocks, begun], "first_group", 8,
    )
    got = [[permute(sent_first[side - 1], "prow", side) for side in sides]]
    outs = call(
        functools.partial(
            second_kernel, near, width, n_col, slab, count, len(sides), late, owns
        ),
        [floats(count * slab, LANES)] * len(sides) + [floats(slab, LANES)] * len(owns),
        [w_split, blocks, begun, data], "second_group_and_own_side", 40,
        [VMEM] * 3 + [HBM],
        [
            pltpu.VMEM((len(owns), rows, width), jnp.float32),
            pltpu.SemaphoreType.DMA((len(owns), n_col)),
        ],
    )
    sent_second, own = outs[: len(sides)], outs[len(sides) :]
    got.append([permute(sent_second[side - 1], "prow", side) for side in sides])
    parts = []
    for index, group in enumerate(groups):
        gram_sent = index == 0
        sums = call(
            functools.partial(side_sum_kernel, count, slab, len(sides), gram_sent),
            [floats(slab + GRAM_ROWS, LANES)] * count + [floats(GRAM_ROWS, LANES)] * gram_sent,
            [*own[index * count : (index + 1) * count], gram, *got[index]], "side_sum",
        )
        if gram_sent:
            *sums, gram = sums
        for turn, value in zip(group, sums):
            parts.append(permute(value, "prow", turn * near) if turn else value)
    fresh = call(
        functools.partial(sweep_kernel, width), floats(n_row, rank, width),
        [*parts, h_prior], "row_sweep",
    )
    pieces = lax.all_to_all(fresh, "prow", 0, 0)
    return call(
        functools.partial(assemble_kernel, width), floats(rank, cols), [pieces], "assemble"
    )


def solution(mesh):
    n_row, n_col = mesh.shape["prow"], mesh.shape["pcol"]
    placed = (P("prow", "pcol"), P(None, ("prow", "pcol")), P(None, "pcol"))
    return jax.shard_map(
        functools.partial(shards, n_row, n_col),
        mesh=mesh, in_specs=placed, out_specs=P(None, "pcol"), check_vma=False,
    )
```

profile of v0, /device:TPU:0, one launch (start us, length us, event | category | flops | bytes accessed | tf_op | source)
XLA Modules:
  0.0 36.9 jit_solution(3194780006994480738)
XLA Ops:
  0.0 0.0 copy-start.1
  0.0 0.5 %collective-permute-start.2 = (f32[32,512]{1,0:T(8,128)}, f32[32,512]{1,0:T(8,128)S(1)}, u32[]{:S(2)}, u32[]{:S(2)}) collective-permute-start(f32[32,512]{1,0:T(8,128)} %refs_0_.1), channel_id=1, source_target_pairs={{0,1},{1,0},{2,3},{3,2},{4,5},{5,4},{6,7},{7,6},{8,9},{9,8},{10,11... | collective-permute-start | bytes 196616 | tf_op jit(solution)/shard_map/ppermute | solution.py:237
  0.5 2.6 %collective-permute-start.1 = (f32[32,512]{1,0:T(8,128)}, f32[32,512]{1,0:T(8,128)S(1)}, u32[]{:S(2)}, u32[]{:S(2)}) collective-permute-start(f32[32,512]{1,0:T(8,128)} %refs_0_.1), channel_id=1, source_target_pairs={{0,3},{1,2},{2,1},{3,0},{4,7},{5,6},{6,5},{7,4},{8,11},{9,10},{10,... | collective-permute-start | bytes 196616 | tf_op jit(solution)/shard_map/ppermute | solution.py:237
  3.1 0.1 collective-permute-start
  3.1 0.0 collective-permute-done.2.refs_0_
  3.1 3.7 %load_other_side.1 = (f32[4,2048,256]{2,1,0:T(8,128)S(1)}, f32[4,64,128]{2,1,0:T(8,128)S(1)}, bf16[4,64,512]{2,1,0:T(8,128)(2,1)S(1)}, f32[32,32]{1,0:T(8,128)S(1)}) custom-call(f32[32,512]{1,0:T(8,128)S(1)} %collective-permute-done.2.refs_0_, f32[2048,2048]{1,0:T(8,128)} %refs_3_.1), custom_call_target="tpu_custom_call" | custom-call | bytes 16777216 | tf_op jit(solution)/shard_map/load_other_side/pallas_call | solution.py:18
  6.8 0.0 collective-permute-done.1.refs_2_
  6.8 0.7 %collective-permute-done.refs_1_ = f32[32,512]{1,0:T(8,128)S(1)} collective-permute-done((f32[32,512]{1,0:T(8,128)}, f32[32,512]{1,0:T(8,128)S(1)}, u32[]{:S(2)}, u32[]{:S(2)}) %collective-permute-start) | collective-permute-done | bytes 65568 | tf_op jit(solution)/shard_map/ppermute | solution.py:237
  7.5 0.0 copy-done.1
  7.5 0.0 copy-start
  7.5 0.8 %first_group.1 = (f32[136,128]{1,0:T(8,128)S(1)}, bf16[4,64,512]{2,1,0:T(8,128)(2,1)S(1)}, f32[8,128]{1,0:T(8,128)S(1)}) custom-call(f32[32,512]{1,0:T(8,128)S(1)} %copy-done.1, f32[32,512]{1,0:T(8,128)S(1)} %collective-permute-done.refs_1_, f32[32,512]{1,0:T(8,128)S(1)} %collective-permute-done.1.refs_2_, ...), custom_call_target="tpu_custom_call" | custom-call | tf_op jit(solution)/shard_map/first_group/pallas_call | solution.py:18
  8.4 1.6 %collective-permute-start.3 = (f32[136,128]{1,0:T(8,128)S(1)}, f32[136,128]{1,0:T(8,128)S(1)}, u32[]{:S(2)}, u32[]{:S(2)}) collective-permute-start(f32[136,128]{1,0:T(8,128)S(1)} %get-tuple-element.30), channel_id=1, source_target_pairs={{0,4},{4,0},{8,12},{12,8},{16,20},{20,16},{24,28},{28,24},{1,5},{5... | collective-permute-start | bytes 208904 | tf_op jit(solution)/shard_map/ppermute | solution.py:237
  9.9 4.5 %second_group_and_own_side.1 = (f32[128,128]{1,0:T(8,128)S(1)}, f32[64,128]{1,0:T(8,128)S(1)}, f32[64,128]{1,0:T(8,128)S(1)}, f32[64,128]{1,0:T(8,128)S(1)}, f32[64,128]{1,0:T(8,128)S(1)}) custom-call(bf16[4,64,512]{2,1,0:T(8,128)(2,1)S(1)} %get-tuple-element.26.refs_0_, f32[4,2048,256]{2,1,0:T(8,128)S(1)} %get-tuple-element.24.refs_5_.refs_1_, ...), custom_call_target="tpu_custom_call" | custom-call | tf_op jit(solution)/shard_map/second_group_and_own_side/pallas_call | solution.py:18
  14.4 0.6 %collective-permute-start.6 = (f32[128,128]{1,0:T(8,128)S(1)}, f32[128,128]{1,0:T(8,128)S(1)}, u32[]{:S(2)}, u32[]{:S(2)}) collective-permute-start(f32[128,128]{1,0:T(8,128)S(1)} %get-tuple-element.36), channel_id=1, source_target_pairs={{0,4},{4,0},{8,12},{12,8},{16,20},{20,16},{24,28},{28,24},{1,5},{5... | collective-permute-start | bytes 196616 | tf_op jit(solution)/shard_map/ppermute | solution.py:237
  15.0 0.0 collective-permute-done.3.refs_3_
  15.0 2.7 %collective-permute-start.4 = (f32[72,128]{1,0:T(8,128)S(1)}, f32[72,128]{1,0:T(8,128)S(1)}, u32[]{:S(2)}, u32[]{:S(2)}) collective-permute-start(f32[72,128]{1,0:T(8,128)S(1)} %get-tuple-element.31), channel_id=1, source_target_pairs={{0,16},{4,20},{8,24},{12,28},{16,0},{20,4},{24,8},{28,12},{1,17},{... | collective-permute-start | bytes 110600 | tf_op jit(solution)/shard_map/ppermute | solution.py:237
  17.7 1.3 %collective-permute-start.5 = (f32[72,128]{1,0:T(8,128)S(1)}, f32[72,128]{1,0:T(8,128)S(1)}, u32[]{:S(2)}, u32[]{:S(2)}) collective-permute-start(f32[72,128]{1,0:T(8,128)S(1)} %get-tuple-element.32), channel_id=1, source_target_pairs={{0,24},{4,28},{8,16},{12,20},{16,8},{20,12},{24,0},{28,4},{1,25},{... | collective-permute-start | bytes 110600 | tf_op jit(solution)/shard_map/ppermute | solution.py:237
  19.0 0.0 collective-permute-done.6.refs_3_
  19.0 1.4 %collective-permute-start.7 = (f32[72,128]{1,0:T(8,128)S(1)}, f32[72,128]{1,0:T(8,128)S(1)}, u32[]{:S(2)}, u32[]{:S(2)}) collective-permute-start(f32[72,128]{1,0:T(8,128)S(1)} %get-tuple-element.37), channel_id=1, source_target_pairs={{0,8},{4,12},{8,0},{12,4},{16,24},{20,28},{24,16},{28,20},{1,9},{5... | collective-permute-start | bytes 110600 | tf_op jit(solution)/shard_map/ppermute | solution.py:237
  20.4 0.0 collective-permute-done.4.refs_0_
  20.4 3.0 %collective-permute-done.5.refs_1_ = f32[72,128]{1,0:T(8,128)S(1)} collective-permute-done((f32[72,128]{1,0:T(8,128)S(1)}, f32[72,128]{1,0:T(8,128)S(1)}, u32[]{:S(2)}, u32[]{:S(2)}) %collective-permute-start.5) | collective-permute-done | bytes 36896 | tf_op jit(solution)/shard_map/ppermute | solution.py:237
  23.4 0.0 collective-permute-done.7.refs_2_
  23.4 0.0 copy-done
  23.4 0.5 %row_sweep.1 = f32[8,32,256]{2,1,0:T(8,128)S(1)} custom-call(f32[72,128]{1,0:T(8,128)S(1)} %collective-permute-done.4.refs_0_, f32[72,128]{1,0:T(8,128)S(1)} %collective-permute-done.5.refs_1_, f32[72,128]{1,0:T(8,128)S(1)} %collective-permute-done.7.refs_2_, f32[72,128]{1,0:T(8,128)S(1)} %get-tuple-element.38.refs_3_, f32[32,2048]{1,0:T(8,128)S(1)} %copy-done), custom_call_target="tpu_custom_call" | custom-call | tf_op jit(solution)/shard_map/row_sweep/pallas_call | solution.py:18
  23.9 12.3 %all_to_all.5.pieces = f32[8,32,256]{2,1,0:T(8,128)S(1)} all-to-all(f32[8,32,256]{2,1,0:T(8,128)S(1)} %row_sweep.1), channel_id=1, replica_groups=mesh['prow'=8,'pcol'=4] {'prow'}, dimensions={0} | all-to-all | bytes 524288 | tf_op jit(solution)/shard_map/all_to_all | solution.py:296
  36.2 0.7 %assemble.1 = f32[32,2048]{1,0:T(8,128)} custom-call(f32[8,32,256]{2,1,0:T(8,128)S(1)} %all_to_all.5.pieces), custom_call_target="tpu_custom_call" | custom-call | tf_op jit(solution)/shard_map/assemble/pallas_call | solution.py:18
  (2 shorter events, 0.0 us)
Async XLA Ops:
  0.0 7.5 %copy-start.1 = (f32[32,512]{1,0:T(8,128)S(1)}, f32[32,512]{1,0:T(8,128)}, u32[]{:S(2)}) copy-start(f32[32,512]{1,0:T(8,128)} %refs_0_.1) | copy-start | bytes 196612
  0.0 3.1 %collective-permute-start.2 = (f32[32,512]{1,0:T(8,128)}, f32[32,512]{1,0:T(8,128)S(1)}, u32[]{:S(2)}, u32[]{:S(2)}) collective-permute-start(f32[32,512]{1,0:T(8,128)} %refs_0_.1), channel_id=1, source_target_pairs={{0,1},{1,0},{2,3},{3,2},{4,5},{5,4},{6,7},{7,6},{8,9},{9,8},{10,11... | collective-permute-start | bytes 196616 | tf_op jit(solution)/shard_map/ppermute | solution.py:237
  0.5 6.4 %collective-permute-start.1 = (f32[32,512]{1,0:T(8,128)}, f32[32,512]{1,0:T(8,128)S(1)}, u32[]{:S(2)}, u32[]{:S(2)}) collective-permute-start(f32[32,512]{1,0:T(8,128)} %refs_0_.1), channel_id=1, source_target_pairs={{0,3},{1,2},{2,1},{3,0},{4,7},{5,6},{6,5},{7,4},{8,11},{9,10},{10,... | collective-permute-start | bytes 196616 | tf_op jit(solution)/shard_map/ppermute | solution.py:237
  3.1 4.5 %collective-permute-start = (f32[32,512]{1,0:T(8,128)}, f32[32,512]{1,0:T(8,128)S(1)}, u32[]{:S(2)}, u32[]{:S(2)}) collective-permute-start(f32[32,512]{1,0:T(8,128)} %refs_0_.1), channel_id=1, source_target_pairs={{0,2},{1,3},{2,0},{3,1},{4,6},{5,7},{6,4},{7,5},{8,10},{9,11},{10,... | collective-permute-start | bytes 196616 | tf_op jit(solution)/shard_map/ppermute | solution.py:237
  7.5 15.9 %copy-start = (f32[32,2048]{1,0:T(8,128)S(1)}, f32[32,2048]{1,0:T(8,128)}, u32[]{:S(2)}) copy-start(f32[32,2048]{1,0:T(8,128)} %refs_4_.1) | copy-start | bytes 786436
  8.4 6.6 %collective-permute-start.3 = (f32[136,128]{1,0:T(8,128)S(1)}, f32[136,128]{1,0:T(8,128)S(1)}, u32[]{:S(2)}, u32[]{:S(2)}) collective-permute-start(f32[136,128]{1,0:T(8,128)S(1)} %get-tuple-element.30), channel_id=1, source_target_pairs={{0,4},{4,0},{8,12},{12,8},{16,20},{20,16},{24,28},{28,24},{1,5},{5... | collective-permute-start | bytes 208904 | tf_op jit(solution)/shard_map/ppermute | solution.py:237
  14.4 4.6 %collective-permute-start.6 = (f32[128,128]{1,0:T(8,128)S(1)}, f32[128,128]{1,0:T(8,128)S(1)}, u32[]{:S(2)}, u32[]{:S(2)}) collective-permute-start(f32[128,128]{1,0:T(8,128)S(1)} %get-tuple-element.36), channel_id=1, source_target_pairs={{0,4},{4,0},{8,12},{12,8},{16,20},{20,16},{24,28},{28,24},{1,5},{5... | collective-permute-start | bytes 196616 | tf_op jit(solution)/shard_map/ppermute | solution.py:237
  15.0 5.4 %collective-permute-start.4 = (f32[72,128]{1,0:T(8,128)S(1)}, f32[72,128]{1,0:T(8,128)S(1)}, u32[]{:S(2)}, u32[]{:S(2)}) collective-permute-start(f32[72,128]{1,0:T(8,128)S(1)} %get-tuple-element.31), channel_id=1, source_target_pairs={{0,16},{4,20},{8,24},{12,28},{16,0},{20,4},{24,8},{28,12},{1,17},{... | collective-permute-start | bytes 110600 | tf_op jit(solution)/shard_map/ppermute | solution.py:237
  17.7 5.8 %collective-permute-start.5 = (f32[72,128]{1,0:T(8,128)S(1)}, f32[72,128]{1,0:T(8,128)S(1)}, u32[]{:S(2)}, u32[]{:S(2)}) collective-permute-start(f32[72,128]{1,0:T(8,128)S(1)} %get-tuple-element.32), channel_id=1, source_target_pairs={{0,24},{4,28},{8,16},{12,20},{16,8},{20,12},{24,0},{28,4},{1,25},{... | collective-permute-start | bytes 110600 | tf_op jit(solution)/shard_map/ppermute | solution.py:237
  19.0 4.4 %collective-permute-start.7 = (f32[72,128]{1,0:T(8,128)S(1)}, f32[72,128]{1,0:T(8,128)S(1)}, u32[]{:S(2)}, u32[]{:S(2)}) collective-permute-start(f32[72,128]{1,0:T(8,128)S(1)} %get-tuple-element.37), channel_id=1, source_target_pairs={{0,8},{4,12},{8,0},{12,4},{16,24},{20,28},{24,16},{28,20},{1,9},{5... | collective-permute-start | bytes 110600 | tf_op jit(solution)/shard_map/ppermute | solution.py:237
where the time goes:
time: 37.1 us; the launch traced here: 36.9 us
  blocking collectives  12.3 us (33%)
  starting transfers between devices  10.6 us (29%)
  Pallas kernels  10.2 us (27%)
  waiting for transfers between devices  3.74 us (10%)
    all_to_all x1, blocking collectives, shards(): pieces = lax.all_to_all(fresh, 'prow', 0, 0)  12.3 us
    ppermute x8, starting transfers between devices, permute(): return lax.ppermute(value, axis, [(i, i ^ turn) for i in range(size)])  10.6 us
    pallas_call x7, Pallas kernels, call(): pl.pallas_call(kernel, out_shape=out_shape, in_specs=in_specs or [VMEM] *...  10.2 us
    ppermute x8, waiting for transfers between devices, permute(): return lax.ppermute(value, axis, [(i, i ^ turn) for i in range(size)])  3.74 us
  transfers between devices with their start and end apart: 8, of which 2 were waited for; matrix products, arithmetic and copies ran while one was open for 0% of the time, Pallas kernels for 22%

commit v1 on v0

v1 whole, which is shorter than its diff:
```python
import functools

import jax
import jax.numpy as jnp
from jax import lax
from jax.experimental import pallas as pl
from jax.experimental.pallas import tpu as pltpu
from jax.sharding import PartitionSpec as P

LANES = 128
GRAM_ROWS = 8
VMEM = pl.BlockSpec(memory_space=pltpu.VMEM)
HBM = pl.BlockSpec(memory_space=pltpu.HBM)


def call(kernel, out_shape, operands, name, mebibytes=4, in_specs=None, scratch=(), cost=None):
    many = isinstance(out_shape, list)
    return pl.pallas_call(
        kernel,
        out_shape=out_shape,
        in_specs=in_specs or [VMEM] * len(operands),
        out_specs=[VMEM] * len(out_shape) if many else VMEM,
        compiler_params=pltpu.CompilerParams(vmem_limit_bytes=mebibytes * 1024 * 1024),
        scratch_shapes=list(scratch),
        cost_estimate=cost,
        name=name,
    )(*operands)


def floats(*shape):
    return jax.ShapeDtypeStruct(shape, jnp.float32)


def split(value):
    high = value.astype(jnp.bfloat16)
    low = (value - high.astype(jnp.float32)).astype(jnp.bfloat16)
    return high, low


def exact_dot(left, right, dims):
    return lax.dot_general(
        left, right, (dims, ((), ())),
        precision=lax.Precision.HIGHEST, preferred_element_type=jnp.float32,
    )


def block_start(near, width, side_turn, level_turn):
    row_at = lax.axis_index("prow")
    side, level = lax.rem(row_at, near), lax.div(row_at, near)
    peer = (level ^ level_turn) * near + (side ^ side_turn)
    return pl.multiple_of(peer * width, width)


def row_part(depth, turn):
    return pl.ds(pl.multiple_of((lax.axis_index("pcol") ^ turn) * depth, depth), depth)


def block_copies(near, width, n_col, order, data_ref, out_ref, sems):
    depth = data_ref.shape[0] // n_col
    copies = {}
    for (at, turns), turn in order:
        columns = pl.ds(block_start(near, width, *turns), width)
        rows = row_part(depth, turn)
        copies[at, turn] = pltpu.make_async_copy(
            data_ref.at[rows, columns], out_ref.at[at, rows], sems.at[at, turn]
        )
    return copies


def split_basis(part_refs, out_ref):
    gram = None
    for at, part_ref in enumerate(part_refs):
        rank = part_ref.shape[0]
        part = part_ref[...]
        high, low = split(part)
        out_ref[at, :rank] = high
        out_ref[at, rank:] = low
        own = exact_dot(part, part, ((1,), (1,)))
        gram = own if gram is None else gram + own
    return gram


def product(basis, blocks, at):
    total = None
    for turn, part_ref, index in basis:
        rank, depth = part_ref.shape[1] // 2, part_ref.shape[2]
        high, low = split(blocks[at, row_part(depth, turn)])
        upper = jnp.dot(part_ref[index], high, preferred_element_type=jnp.float32)
        term = (
            upper[:rank]
            + upper[rank:]
            + jnp.dot(part_ref[index, :rank], low, preferred_element_type=jnp.float32)
        )
        total = term if total is None else total + term
    return total


def parts_of(turns, part_ref):
    return [(turn, part_ref, index) for index, turn in enumerate(turns)]


def store(cross, out_ref, row, before=None):
    rank = cross.shape[0]
    for i in range(cross.shape[1] // LANES):
        rows = slice(row + rank * i, row + rank * (i + 1))
        piece = cross[:, LANES * i : LANES * (i + 1)]
        out_ref[rows] = piece if before is None else piece + before[rows]


def own_region(compute):
    pl.when(lax.axis_index("prow") >= 0)(compute)


def add_to(cross, out_ref, row, before):
    store(cross, out_ref.at[pl.ds(row, before.shape[0])], 0, before)


def load_kernel(near, width, n_col, stages, others, *refs):
    first = stages[0]
    w_refs, data_ref = refs[: len(first)], refs[len(first)]
    blocks, begun, w_split, gram_ref, sems = refs[len(first) + 1 :]
    order = [(at, turn) for stage in stages for turn in stage for at in enumerate(others)]
    copies = block_copies(near, width, n_col, order, data_ref, blocks, sems)
    for copy in copies.values():
        copy.start()

    def compute():
        gram_ref[...] = split_basis(w_refs, w_split)
        for at in range(len(others)):
            for turn in first:
                copies[at, turn].wait()
            store(product(parts_of(first, w_split), blocks, at), begun.at[at], 0)

    own_region(compute)
    for (_, turn), copy in copies.items():
        if turn not in first:
            copy.wait()


def relay_kernel(*refs):
    count = len(refs) // 2
    for ref, out_ref in zip(refs[:count], refs[count + 1 :]):
        out_ref[...] = ref[...]


def middle_kernel(near, width, n_col, turns, own, *refs):
    w_refs, (gram_before, blocks, begun, data_ref) = refs[: len(turns)], refs[len(turns) :][:4]
    further, w_split, gram_ref, own_block, sems = refs[len(turns) + 4 :]
    order = [((0, own), turn) for turn in range(n_col)]
    copies = block_copies(near, width, n_col, order, data_ref, own_block, sems)
    for copy in copies.values():
        copy.start()

    def compute():
        gram_ref[...] = gram_before[...] + split_basis(w_refs, w_split)
        for at in range(blocks.shape[0]):
            add_to(
                product(parts_of(turns, w_split), blocks, at), further.at[at], 0, begun.at[at]
            )

    own_region(compute)
    for copy in copies.values():
        copy.wait()


def first_group_kernel(slab, count, turns, *refs):
    w_refs, (gram_before, blocks, further) = refs[: len(turns)], refs[len(turns) :][:3]
    *out_refs, w_split, gram_ref = refs[len(turns) + 3 :]
    gram = gram_before[...] + split_basis(w_refs, w_split)
    slabs = [gram[GRAM_ROWS * i : GRAM_ROWS * (i + 1)] for i in range(gram.shape[0] // GRAM_ROWS)]
    packed = jnp.concatenate(slabs, axis=1)
    gram_ref[...] = packed
    for index, out_ref in enumerate(out_refs):
        for at in range(count):
            block = index * count + at
            add_to(
                product(parts_of(turns, w_split), blocks, block), out_ref, slab * at,
                further.at[block],
            )
        out_ref[slab * count :] = packed


def second_group_kernel(near, width, n_col, slab, count, n_sides, stages, owns, *refs):
    w_refs, (blocks, further, own_block, data_ref) = refs[:3], refs[3:7]
    out_refs, (own_ref, rest, sems) = refs[7 : 7 + n_sides], refs[7 + n_sides :]
    basis = [part for turns, ref in zip(stages, w_refs) for part in parts_of(turns, ref)]
    order = [(at, turn) for at in enumerate(owns[1:]) for turn in range(n_col)]
    copies = block_copies(near, width, n_col, order, data_ref, rest, sems)
    for copy in copies.values():
        copy.start()

    def compute():
        for index, out_ref in enumerate(out_refs):
            for at in range(count):
                block = (n_sides + index) * count + at
                add_to(
                    product(parts_of(stages[2], w_refs[2]), blocks, block), out_ref, slab * at,
                    further.at[block],
                )
        store(product(basis, own_block, 0), own_ref.at[0], 0)

    def multiply(at):
        for turn in range(n_col):
            copies[at, turn].wait()
        store(product(basis, rest, at), own_ref.at[at + 1], 0)

    own_region(compute)
    for at in range(len(owns) - 2):
        own_region(functools.partial(multiply, at))
    for turn in range(n_col):
        copies[len(owns) - 2, turn].wait()


def last_block_kernel(stages, *refs):
    w_refs, rest, out_ref = refs[:3], refs[3], refs[4]
    basis = [part for turns, ref in zip(stages, w_refs) for part in parts_of(turns, ref)]
    store(product(basis, rest, rest.shape[0] - 1), out_ref, 0)


def side_sum_kernel(slab, levels, gram_sent, n_got, *refs):
    count = len(levels)
    own_refs, gram_ref, got_refs = refs[:count], refs[count], refs[count + 1 : count + 1 + n_got]
    out_refs = refs[count + 1 + n_got :]
    gram = gram_ref[...]
    if gram_sent:
        for got in got_refs:
            gram = gram + got[slab * count :]
        out_refs[count][...] = gram
    for at, level in enumerate(levels):
        total = own_refs[at][...] if level is None else own_refs[at][level]
        for got in got_refs:
            total = total + got[slab * at : slab * (at + 1)]
        out_refs[at][:slab] = total
        out_refs[at][slab:] = gram


def sweep_kernel(width, *refs):
    parts, h_ref, out_ref = refs[:-2], refs[-2], refs[-1]
    rank = h_ref.shape[0]
    row_at = lax.axis_index("prow")
    total = parts[0][...]
    for part in parts[1:]:
        total = total + part[...]
    pieces = width // LANES
    cross = jnp.concatenate([total[rank * i : rank * (i + 1)] for i in range(pieces)], axis=1)
    packed = total[rank * pieces :]
    gram = jnp.concatenate(
        [packed[:, rank * i : rank * (i + 1)] for i in range(rank // GRAM_ROWS)], axis=0
    )
    h = h_ref[:, pl.ds(pl.multiple_of(row_at * width, width), width)]
    rest = cross - exact_dot(gram, h, ((1,), (0,)))
    rows = []
    for k in range(rank):
        inverse = 1.0 / gram[k : k + 1, k : k + 1]
        old = h[k : k + 1]
        fresh = jnp.maximum(old + rest[k : k + 1] * inverse, 0.0)
        rows.append(fresh)
        rest = rest - gram[:, k : k + 1] * (fresh - old)
    done = jnp.concatenate(rows, axis=0)
    for peer in range(out_ref.shape[0]):
        out_ref[peer] = done


def assemble_kernel(width, pieces, out_ref):
    for peer in range(pieces.shape[0]):
        out_ref[:, width * peer : width * (peer + 1)] = pieces[peer]


def shards(n_row, n_col, data, w_trans, h_prior):
    rank, depth = w_trans.shape
    rows, cols = data.shape
    width = cols // n_row
    near = max(1, n_row // 4)
    far = n_row // near
    slab = rank * (width // LANES)
    count = far // 2
    groups = [list(range(far - 1, count - 1, -1)), list(range(count - 1, -1, -1))]
    sides = range(1, near)

    def permute(value, axis, turn):
        size = n_row if axis == "prow" else n_col
        return lax.ppermute(value, axis, [(i, i ^ turn) for i in range(size)])

    stages = [[1], list(range(0, n_col, 2)), list(range(3, n_col, 2))]
    w_parts = {1: permute(w_trans, "pcol", 1), 0: w_trans}
    for turn in stages[1][1:]:
        w_parts[turn] = permute(w_trans, "pcol", turn)
    others = [(side, turn) for group in groups for side in sides for turn in group]
    owns = [(0, turn) for group in groups for turn in group]

    def split_parts(stage):
        return jax.ShapeDtypeStruct((len(stage), 2 * rank, depth), jnp.bfloat16)

    def semaphores(count):
        return pltpu.SemaphoreType.DMA((count, n_col))

    products = floats(len(others), slab, LANES)
    blocks, begun, w_first, gram = call(
        functools.partial(load_kernel, near, width, n_col, stages, others),
        [floats(len(others), rows, width), products, split_parts(stages[0]), floats(rank, rank)],
        [*(w_parts[t] for t in stages[0]), data], "load_other_side", 40,
        [VMEM] * len(stages[0]) + [HBM], [semaphores(len(others))],
        pl.CostEstimate(
            flops=0, bytes_accessed=8 * rows * width * len(others), transcendentals=0
        ),
    )
    arrived = call(
        relay_kernel, [floats(rank, depth)] * (len(stages[1]) - 1),
        [*(w_parts[t] for t in stages[1][1:]), gram], "relay",
    )
    for turn, value in zip(stages[1][1:], arrived):
        w_parts[turn] = value
        w_parts[turn + 1] = permute(value, "pcol", 1)
    further, w_second, gram, own_block = call(
        functools.partial(middle_kernel, near, width, n_col, stages[1], owns[0]),
        [products, split_parts(stages[1]), floats(rank, rank), floats(1, rows, width)],
        [*(w_parts[t] for t in stages[1]), gram, blocks, begun, data], "middle", 37,
        [VMEM] * (len(stages[1]) + 3) + [HBM], [semaphores(1)],
    )
    *sent_first, w_third, gram = call(
        functools.partial(first_group_kernel, slab, count, stages[2]),
        [floats(count * slab + GRAM_ROWS, LANES)] * len(sides)
        + [split_parts(stages[2]), floats(GRAM_ROWS, LANES)],
        [*(w_parts[t] for t in stages[2]), gram, blocks, further], "first_group", 8,
    )
    w_split = [w_first, w_second, w_third]
    got = [[permute(sent_first[side - 1], "prow", side) for side in sides]]
    *sent_second, own, rest = call(
        functools.partial(
            second_group_kernel, near, width, n_col, slab, count, len(sides), stages, owns
        ),
        [floats(count * slab, LANES)] * len(sides)
        + [floats(far - 1, slab, LANES), floats(far - 1, rows, width)],
        [*w_split, blocks, further, own_block, data], "second_group_and_own_side", 36,
        [VMEM] * 6 + [HBM], [semaphores(far - 1)],
    )
    got.append([permute(sent_second[side - 1], "prow", side) for side in sides])
    last = call(
        functools.partial(last_block_kernel, stages), floats(slab, LANES), [*w_split, rest],
        "last_block", 8,
    )
    parts = []
    for index, group in enumerate(groups):
        gram_sent = index == 0
        levels = [index * count + at for at in range(count)]
        levels = [level if level < far - 1 else None for level in levels]
        sums = call(
            functools.partial(side_sum_kernel, slab, levels, gram_sent, len(sides)),
            [floats(slab + GRAM_ROWS, LANES)] * count + [floats(GRAM_ROWS, LANES)] * gram_sent,
            [*(last if level is None else own for level in levels), gram, *got[index]],
            "side_sum",
        )
        if gram_sent:
            *sums, gram = sums
        for turn, value in zip(group, sums):
            parts.append(permute(value, "prow", turn * near) if turn else value)
    fresh = call(
        functools.partial(sweep_kernel, width), floats(n_row, rank, width),
        [*parts, h_prior], "row_sweep",
    )
    pieces = lax.all_to_all(fresh, "prow", 0, 0)
    return call(
        functools.partial(assemble_kernel, width), floats(rank, cols), [pieces], "assemble"
    )


def solution(mesh):
    n_row, n_col = mesh.shape["prow"], mesh.shape["pcol"]
    placed = (P("prow", "pcol"), P(None, ("prow", "pcol")), P(None, "pcol"))
    return jax.shard_map(
        functools.partial(shards, n_row, n_col),
        mesh=mesh, in_specs=placed, out_specs=P(None, "pcol"), check_vma=False,
    )
```

time: 37.1 us -> 36.9 us (level)
  starting transfers between devices: 10.6 us -> 10.2 us
    ppermute x8, starting transfers between devices: 10.6 us -> 10.2 us  [permute(): return lax.ppermute(value, axis, [(i, i ^ turn) for i in range(size)])]
    pallas_call x7 -> x10, Pallas kernels: 10.2 us -> 10.4 us  [call(): pl.pallas_call(kernel, out_shape=out_shape, in_specs=in_specs or [VMEM] *...]
  transfers between devices with their start and end apart: 8 -> 8, of which waited for: 2 -> 2; matrix products, arithmetic and copies ran while one was open for 0% -> 0% of each run, Pallas kernels for 22% -> 24%
where the time goes in v1:
time: 36.9 us; the launch traced here: 36.7 us
  blocking collectives  12.3 us (33%)
  Pallas kernels  10.4 us (28%)
  starting transfers between devices  10.2 us (28%)
  waiting for transfers between devices  3.72 us (10%)
    all_to_all x1, blocking collectives, shards(): pieces = lax.all_to_all(fresh, 'prow', 0, 0)  12.3 us
    pallas_call x10, Pallas kernels, call(): pl.pallas_call(kernel, out_shape=out_shape, in_specs=in_specs or [VMEM] *...  10.4 us
    ppermute x8, starting transfers between devices, permute(): return lax.ppermute(value, axis, [(i, i ^ turn) for i in range(size)])  10.2 us
    ppermute x8, waiting for transfers between devices, permute(): return lax.ppermute(value, axis, [(i, i ^ turn) for i in range(size)])  3.72 us
  transfers between devices with their start and end apart: 8, of which 2 were waited for; matrix products, arithmetic and copies ran while one was open for 0% of the time, Pallas kernels for 24%

profile of v1, /device:TPU:0, one launch (start us, length us, event | category | flops | bytes accessed | tf_op | source)
XLA Modules:
  0.0 36.7 jit_solution(2666732152351429876)
XLA Ops:
  0.0 0.0 copy-start.1
  0.0 0.5 %collective-permute-start = (f32[32,512]{1,0:T(8,128)}, f32[32,512]{1,0:T(8,128)S(1)}, u32[]{:S(2)}, u32[]{:S(2)}) collective-permute-start(f32[32,512]{1,0:T(8,128)} %refs_0_.1), channel_id=1, source_target_pairs={{0,1},{1,0},{2,3},{3,2},{4,5},{5,4},{6,7},{7,6},{8,9},{9,8},{10,11... | collective-permute-start | bytes 196616 | tf_op jit(solution)/shard_map/ppermute | solution.py:282
  0.5 2.5 %collective-permute-start.1 = (f32[32,512]{1,0:T(8,128)}, f32[32,512]{1,0:T(8,128)S(1)}, u32[]{:S(2)}, u32[]{:S(2)}) collective-permute-start(f32[32,512]{1,0:T(8,128)} %refs_0_.1), channel_id=1, source_target_pairs={{0,2},{1,3},{2,0},{3,1},{4,6},{5,7},{6,4},{7,5},{8,10},{9,11},{10,... | collective-permute-start | bytes 196616 | tf_op jit(solution)/shard_map/ppermute | solution.py:282
  3.0 0.0 collective-permute-done.refs_0_
  3.0 3.7 %load_other_side.1 = (f32[4,2048,256]{2,1,0:T(8,128)S(1)}, f32[4,64,128]{2,1,0:T(8,128)S(1)}, bf16[1,64,512]{2,1,0:T(8,128)(2,1)S(1)}, f32[32,32]{1,0:T(8,128)S(1)}) custom-call(f32[32,512]{1,0:T(8,128)S(1)} %collective-permute-done.refs_0_, f32[2048,2048]{1,0:T(8,128)} %refs_6_.1), custom_call_target="tpu_custom_call" | custom-call | bytes 16777216 | tf_op jit(solution)/shard_map/load_other_side/pallas_call | solution.py:18
  6.7 0.0 collective-permute-done.1.refs_0_
  6.8 0.2 collective-permute-start.2
  7.0 0.0 copy-done.1
  7.0 1.6 %middle.1 = (f32[4,64,128]{2,1,0:T(8,128)S(1)}, bf16[2,64,512]{2,1,0:T(8,128)(2,1)S(1)}, f32[32,32]{1,0:T(8,128)S(1)}, f32[1,2048,256]{2,1,0:T(8,128)S(1)}) custom-call(f32[32,512]{1,0:T(8,128)S(1)} %copy-done.1, f32[32,512]{1,0:T(8,128)S(1)} %relay.1.refs_1_, f32[32,32]{1,0:T(8,128)S(1)} %get-tuple-element.25.refs_1_.refs_2_, ...), custom_call_target="tpu_custom_call" | custom-call | tf_op jit(solution)/shard_map/middle/pallas_call | solution.py:18
  8.6 0.0 collective-permute-done.2.refs_0_
  8.6 0.4 %first_group.1 = (f32[136,128]{1,0:T(8,128)S(1)}, bf16[1,64,512]{2,1,0:T(8,128)(2,1)S(1)}, f32[8,128]{1,0:T(8,128)S(1)}) custom-call(f32[32,512]{1,0:T(8,128)S(1)} %collective-permute-done.2.refs_0_, f32[32,32]{1,0:T(8,128)S(1)} %get-tuple-element.29.refs_1_, f32[4,2048,256]{2,1,0:T(8,128)S(1)} %get-tuple-element.26.refs_3_.refs_2_, ...), custom_call_target="tpu_custom_call" | custom-call | tf_op jit(solution)/shard_map/first_group/pallas_call | solution.py:18
  8.9 1.5 %collective-permute-start.3 = (f32[136,128]{1,0:T(8,128)S(1)}, f32[136,128]{1,0:T(8,128)S(1)}, u32[]{:S(2)}, u32[]{:S(2)}) collective-permute-start(f32[136,128]{1,0:T(8,128)S(1)} %get-tuple-element.35), channel_id=1, source_target_pairs={{0,4},{4,0},{8,12},{12,8},{16,20},{20,16},{24,28},{28,24},{1,5},{5... | collective-permute-start | bytes 208904 | tf_op jit(solution)/shard_map/ppermute | solution.py:282
  10.5 0.0 copy-start
  10.5 3.1 %second_group_and_own_side.1 = (f32[128,128]{1,0:T(8,128)S(1)}, f32[3,64,128]{2,1,0:T(8,128)S(1)}, f32[3,2048,256]{2,1,0:T(8,128)S(1)}) custom-call(bf16[1,64,512]{2,1,0:T(8,128)(2,1)S(1)} %get-tuple-element.24.refs_0_, bf16[2,64,512]{2,1,0:T(8,128)(2,1)S(1)} %get-tuple-element.28.refs_1_, bf16[1,64,512]{2,1,0:T(8,128)(2,1)S(1)} %get-tuple-element.31.refs_2_, ...), custom_call_target="tpu_custom_call" | custom-call | tf_op jit(solution)/shard_map/second_group_and_own_side/pallas_call | solution.py:18
  13.5 0.6 %collective-permute-start.6 = (f32[128,128]{1,0:T(8,128)S(1)}, f32[128,128]{1,0:T(8,128)S(1)}, u32[]{:S(2)}, u32[]{:S(2)}) collective-permute-start(f32[128,128]{1,0:T(8,128)S(1)} %get-tuple-element.40), channel_id=1, source_target_pairs={{0,4},{4,0},{8,12},{12,8},{16,20},{20,16},{24,28},{28,24},{1,5},{5... | collective-permute-start | bytes 196616 | tf_op jit(solution)/shard_map/ppermute | solution.py:282
  14.2 0.5 %last_block.1.refs_1_ = f32[64,128]{1,0:T(8,128)S(1)} custom-call(bf16[1,64,512]{2,1,0:T(8,128)(2,1)S(1)} %get-tuple-element.24.refs_0_, bf16[2,64,512]{2,1,0:T(8,128)(2,1)S(1)} %get-tuple-element.28.refs_1_, bf16[1,64,512]{2,1,0:T(8,128)(2,1)S(1)} %get-tuple-element.31.refs_2_, f32[3,2048,256]{2,1,0:T(8,128)S(1)} %get-tuple-element.38.refs_3_), custom_call_target="tpu_custom_call" | custom-call | tf_op jit(solution)/shard_map/last_block/pallas_call | solution.py:18
  14.7 0.0 collective-permute-done.3.refs_3_
  14.7 3.7 %collective-permute-start.4 = (f32[72,128]{1,0:T(8,128)S(1)}, f32[72,128]{1,0:T(8,128)S(1)}, u32[]{:S(2)}, u32[]{:S(2)}) collective-permute-start(f32[72,128]{1,0:T(8,128)S(1)} %get-tuple-element.36), channel_id=1, source_target_pairs={{0,24},{4,28},{8,16},{12,20},{16,8},{20,12},{24,0},{28,4},{1,25},{... | collective-permute-start | bytes 110600 | tf_op jit(solution)/shard_map/ppermute | solution.py:282
  18.4 0.0 collective-permute-start.5
  18.4 0.0 collective-permute-done.6.refs_3_
  18.4 1.1 %collective-permute-start.7 = (f32[72,128]{1,0:T(8,128)S(1)}, f32[72,128]{1,0:T(8,128)S(1)}, u32[]{:S(2)}, u32[]{:S(2)}) collective-permute-start(f32[72,128]{1,0:T(8,128)S(1)} %get-tuple-element.41), channel_id=1, source_target_pairs={{0,8},{4,12},{8,0},{12,4},{16,24},{20,28},{24,16},{28,20},{1,9},{5... | collective-permute-start | bytes 110600 | tf_op jit(solution)/shard_map/ppermute | solution.py:282
  19.5 1.2 %collective-permute-done.4.refs_0_ = f32[72,128]{1,0:T(8,128)S(1)} collective-permute-done((f32[72,128]{1,0:T(8,128)S(1)}, f32[72,128]{1,0:T(8,128)S(1)}, u32[]{:S(2)}, u32[]{:S(2)}) %collective-permute-start.4) | collective-permute-done | bytes 36896 | tf_op jit(solution)/shard_map/ppermute | solution.py:282
  20.7 2.5 %collective-permute-done.5.refs_1_ = f32[72,128]{1,0:T(8,128)S(1)} collective-permute-done((f32[72,128]{1,0:T(8,128)S(1)}, f32[72,128]{1,0:T(8,128)S(1)}, u32[]{:S(2)}, u32[]{:S(2)}) %collective-permute-start.5) | collective-permute-done | bytes 36896 | tf_op jit(solution)/shard_map/ppermute | solution.py:282
  23.2 0.0 collective-permute-done.7.refs_2_
  23.2 0.0 copy-done
  23.2 0.5 %row_sweep.1 = f32[8,32,256]{2,1,0:T(8,128)S(1)} custom-call(f32[72,128]{1,0:T(8,128)S(1)} %collective-permute-done.4.refs_0_, f32[72,128]{1,0:T(8,128)S(1)} %collective-permute-done.5.refs_1_, f32[72,128]{1,0:T(8,128)S(1)} %collective-permute-done.7.refs_2_, f32[72,128]{1,0:T(8,128)S(1)} %get-tuple-element.42.refs_3_, f32[32,2048]{1,0:T(8,128)S(1)} %copy-done), custom_call_target="tpu_custom_call" | custom-call | tf_op jit(solution)/shard_map/row_sweep/pallas_call | solution.py:18
  23.7 12.3 %all_to_all.5.pieces = f32[8,32,256]{2,1,0:T(8,128)S(1)} all-to-all(f32[8,32,256]{2,1,0:T(8,128)S(1)} %row_sweep.1), channel_id=1, replica_groups=mesh['prow'=8,'pcol'=4] {'prow'}, dimensions={0} | all-to-all | bytes 524288 | tf_op jit(solution)/shard_map/all_to_all | solution.py:361
  36.0 0.7 %assemble.1 = f32[32,2048]{1,0:T(8,128)} custom-call(f32[8,32,256]{2,1,0:T(8,128)S(1)} %all_to_all.5.pieces), custom_call_target="tpu_custom_call" | custom-call | tf_op jit(solution)/shard_map/assemble/pallas_call | solution.py:18
  (3 shorter events, 0.0 us)
Async XLA Ops:
  0.0 7.0 %copy-start.1 = (f32[32,512]{1,0:T(8,128)S(1)}, f32[32,512]{1,0:T(8,128)}, u32[]{:S(2)}) copy-start(f32[32,512]{1,0:T(8,128)} %refs_0_.1) | copy-start | bytes 196612
  0.0 3.0 %collective-permute-start = (f32[32,512]{1,0:T(8,128)}, f32[32,512]{1,0:T(8,128)S(1)}, u32[]{:S(2)}, u32[]{:S(2)}) collective-permute-start(f32[32,512]{1,0:T(8,128)} %refs_0_.1), channel_id=1, source_target_pairs={{0,1},{1,0},{2,3},{3,2},{4,5},{5,4},{6,7},{7,6},{8,9},{9,8},{10,11... | collective-permute-start | bytes 196616 | tf_op jit(solution)/shard_map/ppermute | solution.py:282
  0.5 6.3 %collective-permute-start.1 = (f32[32,512]{1,0:T(8,128)}, f32[32,512]{1,0:T(8,128)S(1)}, u32[]{:S(2)}, u32[]{:S(2)}) collective-permute-start(f32[32,512]{1,0:T(8,128)} %refs_0_.1), channel_id=1, source_target_pairs={{0,2},{1,3},{2,0},{3,1},{4,6},{5,7},{6,4},{7,5},{8,10},{9,11},{10,... | collective-permute-start | bytes 196616 | tf_op jit(solution)/shard_map/ppermute | solution.py:282
  6.8 1.8 %collective-permute-start.2 = (f32[32,512]{1,0:T(8,128)S(1)}, f32[32,512]{1,0:T(8,128)S(1)}, u32[]{:S(2)}, u32[]{:S(2)}) collective-permute-start(f32[32,512]{1,0:T(8,128)S(1)} %relay.1.refs_1_), channel_id=1, source_target_pairs={{0,1},{1,0},{2,3},{3,2},{4,5},{5,4},{6,7},{7,6},{8,9},{9,8},{10,11... | collective-permute-start | bytes 196616 | tf_op jit(solution)/shard_map/ppermute | solution.py:282
  8.9 5.7 %collective-permute-start.3 = (f32[136,128]{1,0:T(8,128)S(1)}, f32[136,128]{1,0:T(8,128)S(1)}, u32[]{:S(2)}, u32[]{:S(2)}) collective-permute-start(f32[136,128]{1,0:T(8,128)S(1)} %get-tuple-element.35), channel_id=1, source_target_pairs={{0,4},{4,0},{8,12},{12,8},{16,20},{20,16},{24,28},{28,24},{1,5},{5... | collective-permute-start | bytes 208904 | tf_op jit(solution)/shard_map/ppermute | solution.py:282
  10.5 12.8 %copy-start = (f32[32,2048]{1,0:T(8,128)S(1)}, f32[32,2048]{1,0:T(8,128)}, u32[]{:S(2)}) copy-start(f32[32,2048]{1,0:T(8,128)} %refs_4_.1) | copy-start | bytes 786436
  13.5 4.8 %collective-permute-start.6 = (f32[128,128]{1,0:T(8,128)S(1)}, f32[128,128]{1,0:T(8,128)S(1)}, u32[]{:S(2)}, u32[]{:S(2)}) collective-permute-start(f32[128,128]{1,0:T(8,128)S(1)} %get-tuple-element.40), channel_id=1, source_target_pairs={{0,4},{4,0},{8,12},{12,8},{16,20},{20,16},{24,28},{28,24},{1,5},{5... | collective-permute-start | bytes 196616 | tf_op jit(solution)/shard_map/ppermute | solution.py:282
  14.7 6.0 %collective-permute-start.4 = (f32[72,128]{1,0:T(8,128)S(1)}, f32[72,128]{1,0:T(8,128)S(1)}, u32[]{:S(2)}, u32[]{:S(2)}) collective-permute-start(f32[72,128]{1,0:T(8,128)S(1)} %get-tuple-element.36), channel_id=1, source_target_pairs={{0,24},{4,28},{8,16},{12,20},{16,8},{20,12},{24,0},{28,4},{1,25},{... | collective-permute-start | bytes 110600 | tf_op jit(solution)/shard_map/ppermute | solution.py:282
  18.4 4.9 %collective-permute-start.5 = (f32[72,128]{1,0:T(8,128)S(1)}, f32[72,128]{1,0:T(8,128)S(1)}, u32[]{:S(2)}, u32[]{:S(2)}) collective-permute-start(f32[72,128]{1,0:T(8,128)S(1)} %get-tuple-element.37), channel_id=1, source_target_pairs={{0,16},{4,20},{8,24},{12,28},{16,0},{20,4},{24,8},{28,12},{1,17},{... | collective-permute-start | bytes 110600 | tf_op jit(solution)/shard_map/ppermute | solution.py:282
  18.4 4.8 %collective-permute-start.7 = (f32[72,128]{1,0:T(8,128)S(1)}, f32[72,128]{1,0:T(8,128)S(1)}, u32[]{:S(2)}, u32[]{:S(2)}) collective-permute-start(f32[72,128]{1,0:T(8,128)S(1)} %get-tuple-element.41), channel_id=1, source_target_pairs={{0,8},{4,12},{8,0},{12,4},{16,24},{20,28},{24,16},{28,20},{1,9},{5... | collective-permute-start | bytes 110600 | tf_op jit(solution)/shard_map/ppermute | solution.py:282
